TPU v7x, 128 devices: a whole 4x4x4 slice. The times are simulated.
128 devices in a mesh: row: 8 (over z, y_hi), col: 16 (over y_lo, x, core).
Axes of the slice: x: 4, y: 4 (y_hi: 2, y_lo: 2; y = y_hi * 2 + y_lo), z: 4, core: 2. Of those that a mesh axis runs over, the one named last changes fastest.
Arguments:
- img_learner: bfloat16 [16384, 1152], P(('row', 'col')), may hold values from -0.30859375 to 0.30859375
- txt_learner: bfloat16 [16384, 1152], P(('col', 'row')), may hold values from -0.30859375 to 0.30859375
- img_ref: bfloat16 [16384, 1152], P(('row', 'col')), may hold values from -0.30859375 to 0.30859375
- txt_ref: bfloat16 [16384, 1152], P(('col', 'row')), may hold values from -0.30859375 to 0.30859375
- partner: int32 [16384], P(('row', 'col')), may hold values from 0 to 16383, each once
- synthetic: int32 [16384], P(('row', 'col')), may hold values 0 or 1
- span_ids: int32 [16384], P(('row', 'col')), may hold values from 0 to 63, as said below
Outputs:
- img_grad: bfloat16 [16384, 1152], P(('row', 'col'))
- txt_grad: bfloat16 [16384, 1152], P(('col', 'row'))
- span_weight: float32 [64], replicated
Inputs may be any that keep to these rules, and one draw needn't show every extreme that they name: `span_ids`: every group holds exactly 256 images.
All inputs are finite; a program needn't handle non-finite values. No bound on the sum of `synthetic` on one device may be relied on, other than what follows from the above.
Results may differ from a plain program's by a relative error of at most 0.02.
Values may be sent and summed in bfloat16 or wider, within the bound.
No kernel may reach another device: no remote copies, remote signals or barrier semaphores. Data moves between devices by JAX's collectives and lax.ppermute only.
A program may use at most 64 MiB of HBM per device.

v0:
```python
import functools

import jax
import jax.numpy as jnp
from jax import lax
from jax.experimental import pallas as pl
from jax.experimental.pallas import tpu as pltpu
from jax.sharding import PartitionSpec as P

SPANS = 64
D = 1152
SH = 128
CH = 2 * SH
NT = 8 * SH
NI = 8 * CH
META = 16
REFER = CH + META
ROWS = REFER + CH
GROUP = 256.0
SCALE = 10.0
SHIFT = -5.0
SHARP = 5.0
SYNTH = 0.5
LN2 = 0.6931471805599453
LOG2E = 1.4426950408889634
AXES = ("row", "col")
F32 = jnp.float32
BF16 = jnp.bfloat16
MIB = 1 << 20

FLIPS = ("", "x", "y", "z", "xy", "yz", "zx", "xyz")


def place(index):
    row, col = divmod(index, 16)
    return dict(z=row // 2, y=2 * (row % 2) + col // 8, x=(col // 2) % 4, c=col % 2)


def device(z, y, x, c):
    return (2 * z + y // 2) * 16 + 8 * (y % 2) + 2 * x + c


def pairs(axes, kind):
    out = []
    for index in range(128):
        at = place(index)
        k = at["c"] if kind == "mixed" else kind
        for axis in axes:
            if axis == "c":
                at["c"] ^= 1
            else:
                at[axis] = at[axis] ^ 1 if k == 0 else 3 - at[axis]
        out.append((index, device(**at)))
    return out


def swap(value, axes, kind=0):
    return lax.ppermute(value, AXES, pairs(axes, kind))


VM = pl.BlockSpec(memory_space=pltpu.VMEM)


def params(mib):
    return pltpu.CompilerParams(vmem_limit_bytes=mib * MIB)


def core_index():
    return lax.rem(lax.axis_index("col"), 2)


def payload_kernel(mine_l, mine_r, oimg_l, otxt_l, oimg_r, otxt_r, meta, ometa, out):
    core = core_index()
    for place, mine, images, texts in ((0, mine_l, oimg_l, otxt_l), (REFER, mine_r, oimg_r, otxt_r)):
        out[place : place + SH] = jnp.where(core == 0, mine[...], texts[...])
        out[place + SH : place + CH] = jnp.where(core == 0, images[...], mine[...])
    out[CH:REFER] = jnp.zeros((META, D), BF16)
    row = lax.broadcasted_iota(jnp.int32, (META, SH), 0)
    for side, ref in enumerate((meta, ometa)):
        partner, synth, span = (ref[i : i + 1, :] for i in range(3))
        block = jnp.where(row == 0, lax.shift_right_logical(partner, 7), 0)
        block = jnp.where(row == 1, partner & 127, block)
        block = jnp.where(row == 2, span, block)
        block = jnp.where(row == 3, synth, block)
        out[CH:REFER, side * SH : (side + 1) * SH] = block.astype(F32).astype(BF16)


def payload(mine, others, meta, other_meta):
    estimate = pl.CostEstimate(flops=0, bytes_accessed=1 << 21, transcendentals=0)
    args = [*mine, *others, meta, other_meta]
    return call(payload_kernel, args, [(ROWS, D, BF16)], [], estimate, mib=8)[0]


def after(value, *others):
    return lax.optimization_barrier((value, others))[0]


def cube_near(own):
    return [own] + [swap(own, axis, "mixed") for axis in "xyz"]


def cube_edges(X, Y, Z):
    return [swap(Y, "x", "mixed"), swap(Z, "y", "mixed"), swap(X, "z", "mixed")]


def halves_kernel(yz, zx, learn, refer):
    learn[...] = yz[:REFER]
    refer[...] = zx[REFER:]


def cube_corner(XY, YZ, ZX):
    estimate = pl.CostEstimate(flops=0, bytes_accessed=4 << 20, transcendentals=0)
    outs = [(REFER, D, BF16), (CH, D, BF16)]
    learn, refer = call(halves_kernel, [YZ, ZX], outs, [], estimate)
    return [swap(learn, "x", "mixed"), swap(refer, "y", "mixed")]


def text_base(k, core):
    row, col = lax.axis_index("row"), lax.axis_index("col")
    z, yh = row // 2, lax.rem(row, 2)
    yl, x = col // 8, lax.rem(col // 2, 4)
    y = 2 * yh + yl
    x = 3 - x if "x" in FLIPS[k] else x
    y = 3 - y if "y" in FLIPS[k] else y
    z = 3 - z if "z" in FLIPS[k] else z
    col = 8 * lax.rem(y, 2) + 2 * x + core
    row = 2 * z + y // 2
    return (col * 8 + row) * SH


HALF = slice(0, SH), slice(SH, CH)


def pick(core, g, d, base, rows, half):
    mine, other = HALF[half], HALF[1 - half]
    at = slice(base + mine.start, base + mine.stop), slice(base + other.start, base + other.stop)
    return jnp.where(core == 0, g[at[0], :], d[at[1], :]) if rows == "images" else jnp.where(
        core == 0, d[at[0], :], g[at[1], :]
    )


def lanes(k, h):
    if isinstance(k, int):
        return slice(h * NT + k * SH, h * NT + (k + 1) * SH)
    return pl.ds(pl.multiple_of(h * NT + k * SH, SH), SH)


def product(left, right):
    return lax.dot_general(left, right, (((1,), (1,)), ((), ())), preferred_element_type=F32)


STEP = 32


def fold(value):
    return (value[0:8] + value[8:16]) + (value[16:24] + value[24:32])


def fold_product(value):
    return (value[0:8] * value[8:16]) * (value[16:24] * value[24:32])


def inverse(value):
    guess = pltpu.reciprocal(value, approx=True)
    return guess * (2.0 - value * guess)


def activate(learn, refer, partner, bases, store):
    rows, width = learn.shape
    iota = lax.broadcasted_iota(jnp.int32, (STEP, width), 0).astype(F32)
    positive = jnp.zeros((8, width), F32)
    logs = jnp.zeros((8, width), F32)
    factors = None
    count = 0
    for start in range(0, rows, STEP):
        chunk, inner = divmod(start, SH)
        mask = (partner - (bases[chunk] + inner).astype(F32)) == iota

        def part(ref):
            value = ref[start : start + STEP, :] * (SCALE * LOG2E) + (SHIFT * LOG2E)
            value = jnp.where(mask, -value, value)
            small = jnp.exp2(-jnp.abs(value))
            return value, small, 1.0 + small

        value, small, one = part(learn)
        value_r, _, one_r = part(refer)
        positive = positive + fold(jnp.maximum(value, 0.0) - jnp.maximum(value_r, 0.0))
        terms = fold_product(one), fold_product(one_r)
        factors = terms if factors is None else (factors[0] * terms[0], factors[1] * terms[1])
        count += 4
        if count == 64 or start + STEP == rows:
            logs = logs + (jnp.log(factors[0]) - jnp.log(factors[1]))
            factors, count = None, 0
        sig = jnp.where(value >= 0, 1.0, small) * inverse(one)
        store(start, jnp.where(mask, -sig, sig).astype(BF16))
    return positive * LN2 + logs


STAGES = (
    ((0, 1, 2, 3), [(0, 4, k) for k in range(4)]),
    ((4, 5, 6), [(0, 7, k) for k in (4, 5, 6)]),
    ((), [(4, 7, k) for k in range(4)]),
    ((7,), [(0, 8, 7)] + [(7, 8, k) for k in range(7)]),
)


LOOPS = (True, False, True, False)


def stage_kernel(stage, *refs):
    new, blocks = STAGES[stage]
    refs = list(refs)
    last = stage == len(STAGES) - 1
    if last:
        gs, ds, refs = [(refs[0], refs[1])], [(refs[2], refs[3])], refs[4:]
    else:
        count = len(new)
        gs, ds, refs = [(v, v) for v in refs[:count]], [(v, v) for v in refs[count : 2 * count]], refs[2 * count :]
    if stage > 0:
        refs = refs[len(STATE) :]
    grad, excess, meta, img_l, txt_l, img_r, txt_r = refs[: len(STATE)]
    refs = refs[len(STATE) :]
    if last:
        score, refs = refs[0], refs[1:]
    logits = refs
    core = core_index()
    models = ((0, img_l, txt_l), (0 if last else REFER, img_r, txt_r))
    for k, g, d in zip(new, gs, ds):
        for model, (base, img, txt) in enumerate(models):
            txt[k * SH : (k + 1) * SH] = pick(core, g[model], d[model], base, "texts", 0)
            for h in range(2):
                img[lanes(k, h)] = pick(core, g[model], d[model], base, "images", h)
        for h in range(2):
            block = jnp.where(core == 0, g[0][CH:REFER, HALF[h]], d[0][CH:REFER, HALF[1 - h]])
            meta[:, lanes(k, h)] = block.astype(F32)[0:8]
    bases = [text_base(k, core) for k in range(8)]

    def multiply(block, slot):
        first, end, k = block
        for model, (_, img, txt) in enumerate(models):
            images = jnp.concatenate([img[lanes(k, h), :] for h in range(2)], axis=0)
            logits[2 * slot + model][0 : (end - first) * SH] = product(txt[first * SH : end * SH], images)

    def rest(block, slot):
        first, end, k = block

        def store(start, value):
            row = first * SH + start
            for h in range(2):
                grad[row : row + STEP, lanes(k, h)] = value[:, HALF[h]]

        both = [meta[0:1, lanes(k, h)] * 128.0 + meta[1:2, lanes(k, h)] for h in range(2)]
        rows = slice(0, (end - first) * SH)
        learn, refer = (logits[2 * slot + model].at[rows] for model in range(2))
        total = activate(learn, refer, jnp.concatenate(both, axis=1), bases[first:end], store)
        for h in range(2):
            if first == 0:
                excess[:, lanes(k, h)] = total[:, HALF[h]]
            else:
                excess[:, lanes(k, h)] += total[:, HALF[h]]

    if LOOPS[stage]:
        first, end, _ = blocks[0]
        multiply(blocks[0], 0)

        @pl.loop(0, len(blocks) // 2)
        def _(step):
            k = 2 * step
            multiply((first, end, k + 1), 1)
            rest((first, end, k), 0)
            multiply((first, end, jnp.minimum(k + 2, len(blocks) - 1)), 0)
            rest((first, end, k + 1), 1)

    else:
        multiply(blocks[0], 0)
        for index, block in enumerate(blocks):
            if index + 1 < len(blocks):
                multiply(blocks[index + 1], (index + 1) % 2)
            rest(block, index % 2)
    if last:
        span = lax.broadcasted_iota(jnp.int32, (SPANS, SH), 0).astype(F32)
        table = jnp.zeros((SPANS, SH), F32)
        for start in range(0, NI, SH):
            at = slice(start, start + SH)
            part = jnp.sum(excess[:, at], axis=0, keepdims=True)
            table = table + jnp.where(meta[2:3, at] == span, part, 0.0)
        table = jnp.concatenate([table, jnp.zeros((SH - SPANS, SH), F32)], axis=0)
        result = jnp.sum(jnp.transpose(table), axis=0, keepdims=True)
        score[...] = jnp.broadcast_to(result, score.shape)


def shape(rows, columns, kind):
    return jax.ShapeDtypeStruct((rows, columns), kind)


def call(body, args, outs, scratch, estimate, aliases={}, mib=20):
    return pl.pallas_call(
        body,
        out_shape=tuple(shape(*out) for out in outs),
        in_specs=[VM] * len(args),
        out_specs=(VM,) * len(outs),
        scratch_shapes=[pltpu.VMEM((rows, columns), kind) for rows, columns, kind in scratch],
        input_output_aliases=aliases,
        compiler_params=params(mib),
        cost_estimate=estimate,
    )(*args)


STATE = [
    (NT, NI, BF16),
    (8, NI, F32),
    (8, NI, F32),
    (NI, D, BF16),
    (NT, D, BF16),
    (NI, D, BF16),
    (NT, D, BF16),
]


def run_stage(stage, chunks, state):
    new, blocks = STAGES[stage]
    texts = max(end - first for first, end, _ in blocks) * SH
    pairs_done = sum((end - first) * SH * CH for first, end, _ in blocks)
    estimate = pl.CostEstimate(
        flops=4 * pairs_done * D, bytes_accessed=8 << 20, transcendentals=3 * pairs_done
    )
    last = stage == len(STAGES) - 1
    outs = STATE + ([(8, SH, F32)] if last else [])
    aliases = {len(chunks) + i: i for i in range(len(STATE))} if stage else {}
    scratch = [(texts, CH, F32)] * 4
    args = [*chunks, *(state if stage else [])]
    return call(functools.partial(stage_kernel, stage), args, outs, scratch, estimate, aliases)


def image_kernel(half, grad, txt, out):
    @pl.loop(0, NT // (2 * CH))
    def _(block):
        at = pl.ds(pl.multiple_of(half * NT + block * 2 * CH, CH), 2 * CH)
        rows = pl.ds(pl.multiple_of(block * 2 * CH, CH), 2 * CH)
        out[rows, :] = lax.dot_general(
            grad[:, at], txt[...], (((0,), (0,)), ((), ())), preferred_element_type=F32
        ).astype(BF16)


def image_part(grad, txt, half):
    body = functools.partial(image_kernel, half)
    estimate = pl.CostEstimate(flops=2 * NT * NT * D, bytes_accessed=6 << 20, transcendentals=0)
    return call(body, [grad, txt], [(NT, D, BF16)], [], estimate)[0]


def pair_kernel(mine, other, *outs):
    for k, out in enumerate(outs):
        at = slice(k * SH, (k + 1) * SH)
        out[...] = (mine[at].astype(F32) + other[at].astype(F32)).astype(BF16)


def pair_sum(mine, other):
    estimate = pl.CostEstimate(flops=0, bytes_accessed=8 << 20, transcendentals=0)
    return call(pair_kernel, [mine, other], [(SH, D, BF16)] * 8, [], estimate)


def text_kernel(score, meta, grad, img, *rest):
    *outs, weighted = rest
    weight = jax.nn.sigmoid(SHARP * score[0:1, :] / GROUP)
    column = jnp.transpose(jnp.broadcast_to(weight, (SH, SH)))[0:SPANS]
    span = lax.broadcasted_iota(jnp.int32, (SPANS, SH), 0).astype(F32)
    for start in range(0, NI, SH):
        at = slice(start, start + SH)
        chosen = jnp.where(meta[2:3, at] == span, column, 0.0)
        factor = jnp.sum(chosen, axis=0, keepdims=True)
        factor = factor * jnp.where(meta[3:4, at] == 1.0, SCALE * SYNTH, SCALE)
        weighted[:, at] = (grad[:, at].astype(F32) * factor).astype(BF16)
    for first in (4, 0):
        rows = slice(first * SH, (first + 4) * SH)
        total = jnp.dot(weighted[rows], img[...], preferred_element_type=F32)
        for k in range(4):
            outs[first + k][...] = total[k * SH : (k + 1) * SH].astype(BF16)


def text_part(score, meta, grad, img):
    estimate = pl.CostEstimate(flops=2 * NT * NI * D, bytes_accessed=12 << 20, transcendentals=0)
    outs = [(SH, D, BF16)] * 8
    return call(text_kernel, [score, meta, grad, img], outs, [(NT, NI, BF16)], estimate, mib=24)


def add(*terms):
    return sum(t.astype(F32) for t in terms)


def cube_sum(chunks, kind, *earlier):
    own, X, Y, Z, XY, YZ, ZX, XYZ = chunks
    to_yz = swap(XYZ, "x", kind)
    to_x = [swap(XY, "y", kind), swap(ZX, "z", kind)]
    from_y = swap(after(Y, *earlier), "y", kind)
    X = after(X, to_yz)
    if kind == 1:
        Z = after(Z, to_yz)
    from_z = swap(Z, "z", kind)
    from_yz = swap(add(YZ, to_yz).astype(BF16), "yz", kind)
    from_x = swap(add(X, *to_x).astype(BF16), "x", kind)
    total = add(own, from_yz, from_z)
    rest = after((from_x, from_y), total)
    return add(total, *rest), (from_y, from_z)


def shards(img_learner, txt_learner, img_ref, txt_ref, partner, synthetic, span_ids):
    core = core_index()
    meta = jnp.stack([partner, synthetic, span_ids])
    others = [swap(v, "c") for v in (img_learner, txt_learner, img_ref, txt_ref)]
    mine = [
        jnp.where(core == 0, img_learner, txt_learner),
        jnp.where(core == 0, img_ref, txt_ref),
    ]
    own = payload(mine, others, meta, swap(meta, "c"))
    near = cube_near(own)
    state = run_stage(0, near + [swap(v, "c") for v in near], None)
    edges = cube_edges(*near[1:])
    edges[1] = after(edges[1], state[1])
    corner = cube_corner(*edges)
    state = run_stage(1, edges + [swap(v, "c") for v in edges], state)
    other_corner = [swap(v, "c") for v in after(corner, state[1])]
    state = run_stage(2, [], state)
    *state, partial = run_stage(3, corner + other_corner, state)
    grad, _, meta, img, txt, _, _ = state

    score = partial + swap(partial, "c")
    score = score + swap(score, "x", 0)
    img_send = image_part(grad, after(txt, score), 1)
    score = after(score + swap(score, "x", 1), img_send)
    img_other = swap(after(img_send, score), "c")
    img_keep = image_part(grad, after(txt, score), 0)
    score = after(score + swap(score, "y", 0), img_keep)
    score = score + swap(score, "y", 1)
    img_chunks = pair_sum(img_keep, after(img_other, score))
    score = after(score + swap(score, "z", 0), img_chunks)
    score = score + swap(score, "z", 1)

    txt_chunks = text_part(score, meta, grad, img)
    img_total, img_near = cube_sum(img_chunks, 0, txt_chunks[0])
    txt_total, _ = cube_sum(txt_chunks, 1, img_near[1])
    txt_grad = txt_total.astype(BF16)

    span_weight = jax.nn.sigmoid(SHARP * score[0, :SPANS] / GROUP)
    table = span_ids[:, None] == jnp.arange(SPANS, dtype=jnp.int32)[None, :]
    row_weight = jnp.sum(jnp.where(table, span_weight[None, :], 0.0), axis=1, keepdims=True)
    row_weight = row_weight * jnp.where(synthetic == 1, SCALE * SYNTH, SCALE)[:, None]
    img_grad = (img_total * row_weight).astype(BF16)
    return img_grad, txt_grad, span_weight


def solution(mesh):
    placed = (
        P(("row", "col"), None),
        P(("col", "row"), None),
        P(("row", "col"), None),
        P(("col", "row"), None),
        P(("row", "col")),
        P(("row", "col")),
        P(("row", "col")),
    )
    return jax.shard_map(
        shards,
        mesh=mesh,
        in_specs=placed,
        out_specs=(P(("row", "col"), None), P(("col", "row"), None), P()),
        check_vma=False,
    )
```

profile of v0, /device:TPU:0, one launch (start us, length us, event | category | flops | bytes accessed | tf_op | source)
XLA Modules:
  0.0 130.7 jit_solution(8438762193083345281)
XLA Ops:
  7.9 1.9 %collective-permute-start.5 = (bf16[528,1152]{1,0:T(8,128)(2,1)S(1)}, bf16[528,1152]{1,0:T(8,128)(2,1)S(1)}, u32[]{:S(2)}, u32[]{:S(2)}) collective-permute-start(bf16[528,1152]{1,0:T(8,128)(2,1)S(1)} %shard_map.94.refs_0_), channel_id=1, source_target_pairs={{0,32},{1,97},{2,34},{3,99},{4,36},{5,101},{6,38},{7,103},{8,40},{... | collective-permute-start | bytes 3649544 | tf_op jit(solution)/shard_map/ppermute | solution.py:58
  9.8 4.4 %collective-permute-start.9 = (bf16[528,1152]{1,0:T(8,128)(2,1)S(1)}, bf16[528,1152]{1,0:T(8,128)(2,1)S(1)}, u32[]{:S(2)}, u32[]{:S(2)}) collective-permute-start(bf16[528,1152]{1,0:T(8,128)(2,1)S(1)} %shard_map.94.refs_0_), channel_id=1, source_target_pairs={{0,1},{1,0},{2,3},{3,2},{4,5},{5,4},{6,7},{7,6},{8,9},{9,8},{10,11... | collective-permute-start | bytes 3649544 | tf_op jit(solution)/shard_map/ppermute | solution.py:58
  14.2 7.2 %collective-permute-done.7.refs_1_ = bf16[528,1152]{1,0:T(8,128)(2,1)S(1)} collective-permute-done((bf16[528,1152]{1,0:T(8,128)(2,1)S(1)}, bf16[528,1152]{1,0:T(8,128)(2,1)S(1)}, u32[]{:S(2)}, u32[]{:S(2)}) %collective-permute-start.7) | collective-permute-done | bytes 1216544 | tf_op jit(solution)/shard_map/ppermute | solution.py:58
  24.5 3.7 %collective-permute-start.12 = (bf16[528,1152]{1,0:T(8,128)(2,1)S(1)}, bf16[528,1152]{1,0:T(8,128)(2,1)S(1)}, u32[]{:S(2)}, u32[]{:S(2)}) collective-permute-start(bf16[528,1152]{1,0:T(8,128)(2,1)S(1)} %collective-permute-done.5.refs_3_), channel_id=1, source_target_pairs={{0,1},{1,0},{2,3},{3,2},{4,5},{5,4},{6,7},{7,6},{8,9},{9,8},{10,11... | collective-permute-start | bytes 3649544 | tf_op jit(solution)/shard_map/ppermute | solution.py:58
  28.6 2.1 %collective-permute-done.12.refs_7_ = bf16[528,1152]{1,0:T(8,128)(2,1)S(1)} collective-permute-done((bf16[528,1152]{1,0:T(8,128)(2,1)S(1)}, bf16[528,1152]{1,0:T(8,128)(2,1)S(1)}, u32[]{:S(2)}, u32[]{:S(2)}) %collective-permute-start.12) | collective-permute-done | bytes 1216544 | tf_op jit(solution)/shard_map/ppermute | solution.py:58
  30.7 5.5 %shard_map.95 = (bf16[1024,2048]{1,0:T(8,128)(2,1)S(1)}, f32[8,2048]{1,0:T(8,128)S(1)}, f32[8,2048]{1,0:T(8,128)S(1)}, bf16[2048,1152]{1,0:T(8,128)(2,1)S(1)}, b...) custom-call(bf16[528,1152]{1,0:T(8,128)(2,1)S(1)} %shard_map.94.refs_0_, ...), custom_call_target="tpu_custom_call" | custom-call | flops 2415919104 | bytes 8388608 | tf_op jit(solution)/shard_map/pallas_call | solution.py:297
  36.2 8.5 %collective-permute-done.6.yz.refs_1_ = bf16[528,1152]{1,0:T(8,128)(2,1)S(1)} collective-permute-done((bf16[528,1152]{1,0:T(8,128)(2,1)S(1)}, bf16[528,1152]{1,0:T(8,128)(2,1)S(1)}, u32[]{:S(2)}, u32[]{:S(2)}) %collective-permute-start.6) | collective-permute-done | bytes 1216544 | tf_op jit(solution)/shard_map/ppermute | solution.py:58
  45.3 2.7 %collective-permute-start.17 = (bf16[528,1152]{1,0:T(8,128)(2,1)S(1)}, bf16[528,1152]{1,0:T(8,128)(2,1)S(1)}, u32[]{:S(2)}, u32[]{:S(2)}) collective-permute-start(bf16[528,1152]{1,0:T(8,128)(2,1)S(1)} %collective-permute-done.16.refs_0_), channel_id=1, source_target_pairs={{0,1},{1,0},{2,3},{3,2},{4,5},{5,4},{6,7},{7,6},{8,9},{9,8},{10,11... | collective-permute-start | bytes 3649544 | tf_op jit(solution)/shard_map/ppermute | solution.py:58
  51.1 6.3 %shard_map.97 = (bf16[1024,2048]{1,0:T(8,128)(2,1)S(1)}, f32[8,2048]{1,0:T(8,128)S(1)}, f32[8,2048]{1,0:T(8,128)S(1)}, bf16[2048,1152]{1,0:T(8,128)(2,1)S(1)}, b...) custom-call(bf16[528,1152]{1,0:T(8,128)(2,1)S(1)} %collective-permut, ...), custom_call_target="tpu_custom_call", output_to_operand_aliasing={{0}: (6, {}), {1}: (7, {}), {2}: (8, {}), {3}: (9, {}), {4}... | custom-call | flops 3170893824 | bytes 8388608 | tf_op jit(solution)/shard_map/pallas_call | solution.py:297
  59.3 3.9 %shard_map.98 = (bf16[1024,2048]{1,0:T(8,128)(2,1)S(1)}, f32[8,2048]{1,0:T(8,128)S(1)}, f32[8,2048]{1,0:T(8,128)S(1)}, bf16[2048,1152]{1,0:T(8,128)(2,1)S(1)}, b...) custom-call(bf16[1024,2048]{1,0:T(8,128)(2,1)S(1)} %get-tuple-elemen, ...), custom_call_target="tpu_custom_call", output_to_operand_aliasing={{0}: (0, {}), {1}: (1, {}), {2}: (2, {}), {3}: (3, {}), {4}... | custom-call | flops 1811939328 | bytes 8388608 | tf_op jit(solution)/shard_map/pallas_call | solution.py:297
  63.2 5.5 %shard_map.99 = (bf16[1024,2048]{1,0:T(8,128)(2,1)S(1)}, f32[8,2048]{1,0:T(8,128)S(1)}, f32[8,2048]{1,0:T(8,128)S(1)}, bf16[2048,1152]{1,0:T(8,128)(2,1)S(1)}, b...) custom-call(bf16[272,1152]{1,0:T(8,128)(2,1)S(1)} %collective-permut, ...), custom_call_target="tpu_custom_call", output_to_operand_aliasing={{0}: (4, {}), {1}: (5, {}), {2}: (6, {}), {3}: (7, {}), {4}... | custom-call | flops 2264924160 | bytes 8388608 | tf_op jit(solution)/shard_map/pallas_call | solution.py:297
  71.3 2.4 %collective-permute-done.23 = f32[8,128]{1,0:T(8,128)S(1)} collective-permute-done((f32[8,128]{1,0:T(8,128)S(1)}, f32[8,128]{1,0:T(8,128)S(1)}, u32[]{:S(2)}, u32[]{:S(2)}) %collective-permute-start.23) | collective-permute-done | bytes 4128 | tf_op jit(solution)/shard_map/ppermute | solution.py:58
  75.6 3.2 %shard_map.100 = bf16[1024,1152]{1,0:T(8,128)(2,1)S(1)} custom-call(bf16[1024,2048]{1,0:T(8,128)(2,1)S(1)} %get-tuple-element.92.grad, bf16[1024,1152]{1,0:T(8,128)(2,1)S(1)} %get-tuple-element.97.txt), custom_call_target="tpu_custom_call" | custom-call | flops 2415919104 | bytes 6291456 | tf_op jit(solution)/shard_map/pallas_call | solution.py:297
  78.9 3.2 %shard_map.101.mine = bf16[1024,1152]{1,0:T(8,128)(2,1)S(1)} custom-call(bf16[1024,2048]{1,0:T(8,128)(2,1)S(1)} %get-tuple-element.92.grad, bf16[1024,1152]{1,0:T(8,128)(2,1)S(1)} %get-tuple-element.97.txt), custom_call_target="tpu_custom_call" | custom-call | flops 2415919104 | bytes 6291456 | tf_op jit(solution)/shard_map/pallas_call | solution.py:297
  82.5 2.4 %collective-permute-start.27 = (f32[8,128]{1,0:T(8,128)S(1)}, f32[8,128]{1,0:T(8,128)S(1)}, u32[]{:S(2)}, u32[]{:S(2)}) collective-permute-start(f32[8,128]{1,0:T(8,128)S(1)} %add.73), channel_id=1, source_target_pairs={{0,24},{1,25},{2,26},{3,27},{4,28},{5,29},{6,30},{7,31},{8,16},{9,... | collective-permute-start | bytes 12296 | tf_op jit(solution)/shard_map/ppermute | solution.py:58
  85.0 2.4 %collective-permute-done.27 = f32[8,128]{1,0:T(8,128)S(1)} collective-permute-done((f32[8,128]{1,0:T(8,128)S(1)}, f32[8,128]{1,0:T(8,128)S(1)}, u32[]{:S(2)}, u32[]{:S(2)}) %collective-permute-start.27) | collective-permute-done | bytes 4128 | tf_op jit(solution)/shard_map/ppermute | solution.py:58
  87.4 3.6 %collective-permute-done.34 = f32[8,128]{1,0:T(8,128)S(1)} collective-permute-done((f32[8,128]{1,0:T(8,128)S(1)}, f32[8,128]{1,0:T(8,128)S(1)}, u32[]{:S(2)}, u32[]{:S(2)}) %collective-permute-start.34) | collective-permute-done | bytes 4128 | tf_op jit(solution)/shard_map/ppermute | solution.py:58
  96.5 5.9 %shard_map.103 = (bf16[128,1152]{1,0:T(8,128)(2,1)S(1)}, bf16[128,1152]{1,0:T(8,128)(2,1)S(1)}, bf16[128,1152]{1,0:T(8,128)(2,1)S(1)}, bf16[128,1152]{1,0:T(8,12...) custom-call(f32[8,128]{1,0:T(8,128)S(1)} %add.81.score, ...), custom_call_target="tpu_custom_call" | custom-call | flops 4831838208 | bytes 12582912 | tf_op jit(solution)/shard_map/pallas_call | solution.py:297
  104.0 2.5 %collective-permute-start.40 = (bf16[128,1152]{1,0:T(8,128)(2,1)S(1)}, bf16[128,1152]{1,0:T(8,128)(2,1)S(1)}, u32[]{:S(2)}, u32[]{:S(2)}) collective-permute-start(bf16[128,1152]{1,0:T(8,128)(2,1)S(1)} %get-tuple-element.123), channel_id=1, source_target_pairs={{0,24},{1,25},{2,26},{3,27},{4,28},{5,29},{6,30},{7,31},{8,16},{9,... | collective-permute-start | bytes 884744 | tf_op jit(solution)/shard_map/ppermute | solution.py:58
  111.5 2.8 %collective-permute-done.40 = bf16[128,1152]{1,0:T(8,128)(2,1)S(1)} collective-permute-done((bf16[128,1152]{1,0:T(8,128)(2,1)S(1)}, bf16[128,1152]{1,0:T(8,128)(2,1)S(1)}, u32[]{:S(2)}, u32[]{:S(2)}) %collective-permute-start.40) | collective-permute-done | bytes 294944 | tf_op jit(solution)/shard_map/ppermute | solution.py:58
  115.4 2.5 %collective-permute-start.38 = (bf16[128,1152]{1,0:T(8,128)(2,1)S(1)}, bf16[128,1152]{1,0:T(8,128)(2,1)S(1)}, u32[]{:S(2)}, u32[]{:S(2)}) collective-permute-start(bf16[128,1152]{1,0:T(8,128)(2,1)S(1)} %add_convert_fusion.2), channel_id=1, source_target_pairs={{0,120},{1,121},{2,122},{3,123},{4,124},{5,125},{6,126},{7,127},{8... | collective-permute-start | bytes 884744 | tf_op jit(solution)/shard_map/ppermute | solution.py:58
  120.2 1.9 %collective-permute-start.42 = (bf16[128,1152]{1,0:T(8,128)(2,1)S(1)}, bf16[128,1152]{1,0:T(8,128)(2,1)S(1)}, u32[]{:S(2)}, u32[]{:S(2)}) collective-permute-start(bf16[128,1152]{1,0:T(8,128)(2,1)S(1)} %add_convert_fusion.1), channel_id=1, source_target_pairs={{0,6},{1,7},{2,4},{3,5},{4,2},{5,3},{6,0},{7,1},{8,14},{9,15},{10,... | collective-permute-start | bytes 884744 | tf_op jit(solution)/shard_map/ppermute | solution.py:58
  122.9 2.5 %collective-permute-done.38 = bf16[128,1152]{1,0:T(8,128)(2,1)S(1)} collective-permute-done((bf16[128,1152]{1,0:T(8,128)(2,1)S(1)}, bf16[128,1152]{1,0:T(8,128)(2,1)S(1)}, u32[]{:S(2)}, u32[]{:S(2)}) %collective-permute-start.38) | collective-permute-done | bytes 294944 | tf_op jit(solution)/shard_map/ppermute | solution.py:58
  125.5 4.3 %collective-permute-done.39 = bf16[128,1152]{1,0:T(8,128)(2,1)S(1)} collective-permute-done((bf16[128,1152]{1,0:T(8,128)(2,1)S(1)}, bf16[128,1152]{1,0:T(8,128)(2,1)S(1)}, u32[]{:S(2)}, u32[]{:S(2)}) %collective-permute-start.39) | collective-permute-done | bytes 294944 | tf_op jit(solution)/shard_map/ppermute | solution.py:58
  (100 shorter events, 38.5 us)
Async XLA Ops:
  4.7 16.7 %collective-permute-start.7 = (bf16[528,1152]{1,0:T(8,128)(2,1)S(1)}, bf16[528,1152]{1,0:T(8,128)(2,1)S(1)}, u32[]{:S(2)}, u32[]{:S(2)}) collective-permute-start(bf16[528,1152]{1,0:T(8,128)(2,1)S(1)} %shard_map.94.refs_0_), channel_id=1, source_target_pairs={{0,2},{1,7},{2,0},{3,5},{4,6},{5,3},{6,4},{7,1},{8,10},{9,15},{10,... | collective-permute-start | bytes 3649544 | tf_op jit(solution)/shard_map/ppermute | solution.py:58
  6.3 16.6 %collective-permute-start.8 = (bf16[528,1152]{1,0:T(8,128)(2,1)S(1)}, bf16[528,1152]{1,0:T(8,128)(2,1)S(1)}, u32[]{:S(2)}, u32[]{:S(2)}) collective-permute-start(bf16[528,1152]{1,0:T(8,128)(2,1)S(1)} %shard_map.94.refs_0_), channel_id=1, source_target_pairs={{0,8},{1,25},{2,10},{3,27},{4,12},{5,29},{6,14},{7,31},{8,0},{9,17... | collective-permute-start | bytes 3649544 | tf_op jit(solution)/shard_map/ppermute | solution.py:58
  7.9 16.6 %collective-permute-start.5 = (bf16[528,1152]{1,0:T(8,128)(2,1)S(1)}, bf16[528,1152]{1,0:T(8,128)(2,1)S(1)}, u32[]{:S(2)}, u32[]{:S(2)}) collective-permute-start(bf16[528,1152]{1,0:T(8,128)(2,1)S(1)} %shard_map.94.refs_0_), channel_id=1, source_target_pairs={{0,32},{1,97},{2,34},{3,99},{4,36},{5,101},{6,38},{7,103},{8,40},{... | collective-permute-start | bytes 3649544 | tf_op jit(solution)/shard_map/ppermute | solution.py:58
  9.8 18.5 %collective-permute-start.9 = (bf16[528,1152]{1,0:T(8,128)(2,1)S(1)}, bf16[528,1152]{1,0:T(8,128)(2,1)S(1)}, u32[]{:S(2)}, u32[]{:S(2)}) collective-permute-start(bf16[528,1152]{1,0:T(8,128)(2,1)S(1)} %shard_map.94.refs_0_), channel_id=1, source_target_pairs={{0,1},{1,0},{2,3},{3,2},{4,5},{5,4},{6,7},{7,6},{8,9},{9,8},{10,11... | collective-permute-start | bytes 3649544 | tf_op jit(solution)/shard_map/ppermute | solution.py:58
  28.2 16.6 %collective-permute-start.6 = (bf16[528,1152]{1,0:T(8,128)(2,1)S(1)}, bf16[528,1152]{1,0:T(8,128)(2,1)S(1)}, u32[]{:S(2)}, u32[]{:S(2)}) collective-permute-start(bf16[528,1152]{1,0:T(8,128)(2,1)S(1)} %collective-permute-done.5.refs_3_), channel_id=1, source_target_pairs={{0,8},{1,25},{2,10},{3,27},{4,12},{5,29},{6,14},{7,31},{8,0},{9,17... | collective-permute-start | bytes 3649544 | tf_op jit(solution)/shard_map/ppermute | solution.py:58
  28.3 16.6 %collective-permute-start.13 = (bf16[528,1152]{1,0:T(8,128)(2,1)S(1)}, bf16[528,1152]{1,0:T(8,128)(2,1)S(1)}, u32[]{:S(2)}, u32[]{:S(2)}) collective-permute-start(bf16[528,1152]{1,0:T(8,128)(2,1)S(1)} %collective-permute-done.7.refs_1_), channel_id=1, source_target_pairs={{0,32},{1,97},{2,34},{3,99},{4,36},{5,101},{6,38},{7,103},{8,40},{... | collective-permute-start | bytes 3649544 | tf_op jit(solution)/shard_map/ppermute | solution.py:58
  28.3 17.0 %collective-permute-start.16 = (bf16[528,1152]{1,0:T(8,128)(2,1)S(1)}, bf16[528,1152]{1,0:T(8,128)(2,1)S(1)}, u32[]{:S(2)}, u32[]{:S(2)}) collective-permute-start(bf16[528,1152]{1,0:T(8,128)(2,1)S(1)} %collective-permute-done.8.refs_2_), channel_id=1, source_target_pairs={{0,2},{1,7},{2,0},{3,5},{4,6},{5,3},{6,4},{7,1},{8,10},{9,15},{10,... | collective-permute-start | bytes 3649544 | tf_op jit(solution)/shard_map/ppermute | solution.py:58
  48.1 10.4 %collective-permute-start.14 = (bf16[272,1152]{1,0:T(8,128)(2,1)S(1)}, bf16[272,1152]{1,0:T(8,128)(2,1)S(1)}, u32[]{:S(2)}, u32[]{:S(2)}) collective-permute-start(bf16[272,1152]{1,0:T(8,128)(2,1)S(1)} %get-tuple-element.68), channel_id=1, source_target_pairs={{0,2},{1,7},{2,0},{3,5},{4,6},{5,3},{6,4},{7,1},{8,10},{9,15},{10,... | collective-permute-start | bytes 1880072 | tf_op jit(solution)/shard_map/ppermute | solution.py:58
  48.2 10.1 %collective-permute-start.15 = (bf16[256,1152]{1,0:T(8,128)(2,1)S(1)}, bf16[256,1152]{1,0:T(8,128)(2,1)S(1)}, u32[]{:S(2)}, u32[]{:S(2)}) collective-permute-start(bf16[256,1152]{1,0:T(8,128)(2,1)S(1)} %get-tuple-element.69), channel_id=1, source_target_pairs={{0,8},{1,25},{2,10},{3,27},{4,12},{5,29},{6,14},{7,31},{8,0},{9,17... | collective-permute-start | bytes 1769480 | tf_op jit(solution)/shard_map/ppermute | solution.py:58
  78.7 12.2 %collective-permute-start.25 = (bf16[1024,1152]{1,0:T(8,128)(2,1)S(1)}, bf16[1024,1152]{1,0:T(8,128)(2,1)S(1)}, u32[]{:S(2)}, u32[]{:S(2)}) collective-permute-start(bf16[1024,1152]{1,0:T(8,128)(2,1)S(1)} %shard_map.100), channel_id=1, source_target_pairs={{0,1},{1,0},{2,3},{3,2},{4,5},{5,4},{6,7},{7,6},{8,9},{9,8},{10,11... | collective-permute-start | bytes 7077896 | tf_op jit(solution)/shard_map/ppermute | solution.py:58
  92.8 11.2 %collective-permute-start.30 = (bf16[128,1152]{1,0:T(8,128)(2,1)S(1)}, bf16[128,1152]{1,0:T(8,128)(2,1)S(1)}, u32[]{:S(2)}, u32[]{:S(2)}) collective-permute-start(bf16[128,1152]{1,0:T(8,128)(2,1)S(1)} %get-tuple-element.104), channel_id=1, source_target_pairs={{0,32},{1,33},{2,34},{3,35},{4,36},{5,37},{6,38},{7,39},{8,40},{9,... | collective-permute-start | bytes 884744 | tf_op jit(solution)/shard_map/ppermute | solution.py:58
  93.8 12.7 %collective-permute-start.28 = (bf16[128,1152]{1,0:T(8,128)(2,1)S(1)}, bf16[128,1152]{1,0:T(8,128)(2,1)S(1)}, u32[]{:S(2)}, u32[]{:S(2)}) collective-permute-start(bf16[128,1152]{1,0:T(8,128)(2,1)S(1)} %get-tuple-element.103), channel_id=1, source_target_pairs={{0,2},{1,3},{2,0},{3,1},{4,6},{5,7},{6,4},{7,5},{8,10},{9,11},{10,... | collective-permute-start | bytes 884744 | tf_op jit(solution)/shard_map/ppermute | solution.py:58
  94.0 13.9 %collective-permute-start.31 = (bf16[128,1152]{1,0:T(8,128)(2,1)S(1)}, bf16[128,1152]{1,0:T(8,128)(2,1)S(1)}, u32[]{:S(2)}, u32[]{:S(2)}) collective-permute-start(bf16[128,1152]{1,0:T(8,128)(2,1)S(1)} %get-tuple-element.107), channel_id=1, source_target_pairs={{0,8},{1,9},{2,10},{3,11},{4,12},{5,13},{6,14},{7,15},{8,0},{9,1},... | collective-permute-start | bytes 884744 | tf_op jit(solution)/shard_map/ppermute | solution.py:58
  94.0 14.9 %collective-permute-start.32 = (bf16[128,1152]{1,0:T(8,128)(2,1)S(1)}, bf16[128,1152]{1,0:T(8,128)(2,1)S(1)}, u32[]{:S(2)}, u32[]{:S(2)}) collective-permute-start(bf16[128,1152]{1,0:T(8,128)(2,1)S(1)} %get-tuple-element.108), channel_id=1, source_target_pairs={{0,32},{1,33},{2,34},{3,35},{4,36},{5,37},{6,38},{7,39},{8,40},{9,... | collective-permute-start | bytes 884744 | tf_op jit(solution)/shard_map/ppermute | solution.py:58
  102.3 8.0 %collective-permute-start.37 = (bf16[128,1152]{1,0:T(8,128)(2,1)S(1)}, bf16[128,1152]{1,0:T(8,128)(2,1)S(1)}, u32[]{:S(2)}, u32[]{:S(2)}) collective-permute-start(bf16[128,1152]{1,0:T(8,128)(2,1)S(1)} %get-tuple-element.118), channel_id=1, source_target_pairs={{0,6},{1,7},{2,4},{3,5},{4,2},{5,3},{6,0},{7,1},{8,14},{9,15},{10,... | collective-permute-start | bytes 884744 | tf_op jit(solution)/shard_map/ppermute | solution.py:58
  104.0 10.3 %collective-permute-start.40 = (bf16[128,1152]{1,0:T(8,128)(2,1)S(1)}, bf16[128,1152]{1,0:T(8,128)(2,1)S(1)}, u32[]{:S(2)}, u32[]{:S(2)}) collective-permute-start(bf16[128,1152]{1,0:T(8,128)(2,1)S(1)} %get-tuple-element.123), channel_id=1, source_target_pairs={{0,24},{1,25},{2,26},{3,27},{4,28},{5,29},{6,30},{7,31},{8,16},{9,... | collective-permute-start | bytes 884744 | tf_op jit(solution)/shard_map/ppermute | solution.py:58
  106.5 8.9 %collective-permute-start.41 = (bf16[128,1152]{1,0:T(8,128)(2,1)S(1)}, bf16[128,1152]{1,0:T(8,128)(2,1)S(1)}, u32[]{:S(2)}, u32[]{:S(2)}) collective-permute-start(bf16[128,1152]{1,0:T(8,128)(2,1)S(1)} %get-tuple-element.124), channel_id=1, source_target_pairs={{0,96},{1,97},{2,98},{3,99},{4,100},{5,101},{6,102},{7,103},{8,104... | collective-permute-start | bytes 884744 | tf_op jit(solution)/shard_map/ppermute | solution.py:58
  108.0 12.2 %collective-permute-start.36 = (bf16[128,1152]{1,0:T(8,128)(2,1)S(1)}, bf16[128,1152]{1,0:T(8,128)(2,1)S(1)}, u32[]{:S(2)}, u32[]{:S(2)}) collective-permute-start(bf16[128,1152]{1,0:T(8,128)(2,1)S(1)} %get-tuple-element.114), channel_id=1, source_target_pairs={{0,8},{1,9},{2,10},{3,11},{4,12},{5,13},{6,14},{7,15},{8,0},{9,1},... | collective-permute-start | bytes 884744 | tf_op jit(solution)/shard_map/ppermute | solution.py:58
  108.9 21.0 %collective-permute-start.43 = (bf16[128,1152]{1,0:T(8,128)(2,1)S(1)}, bf16[128,1152]{1,0:T(8,128)(2,1)S(1)}, u32[]{:S(2)}, u32[]{:S(2)}) collective-permute-start(bf16[128,1152]{1,0:T(8,128)(2,1)S(1)} %get-tuple-element.126), channel_id=1, source_target_pairs={{0,24},{1,25},{2,26},{3,27},{4,28},{5,29},{6,30},{7,31},{8,16},{9,... | collective-permute-start | bytes 884744 | tf_op jit(solution)/shard_map/ppermute | solution.py:58
  110.3 8.5 %collective-permute-start.29 = (bf16[128,1152]{1,0:T(8,128)(2,1)S(1)}, bf16[128,1152]{1,0:T(8,128)(2,1)S(1)}, u32[]{:S(2)}, u32[]{:S(2)}) collective-permute-start(bf16[128,1152]{1,0:T(8,128)(2,1)S(1)} %add_convert_fusion.4), channel_id=1, source_target_pairs={{0,40},{1,41},{2,42},{3,43},{4,44},{5,45},{6,46},{7,47},{8,32},{9,... | collective-permute-start | bytes 884744 | tf_op jit(solution)/shard_map/ppermute | solution.py:58
  114.4 7.8 %collective-permute-start.33 = (bf16[128,1152]{1,0:T(8,128)(2,1)S(1)}, bf16[128,1152]{1,0:T(8,128)(2,1)S(1)}, u32[]{:S(2)}, u32[]{:S(2)}) collective-permute-start(bf16[128,1152]{1,0:T(8,128)(2,1)S(1)} %add_convert_fusion.3), channel_id=1, source_target_pairs={{0,2},{1,3},{2,0},{3,1},{4,6},{5,7},{6,4},{7,5},{8,10},{9,11},{10,... | collective-permute-start | bytes 884744 | tf_op jit(solution)/shard_map/ppermute | solution.py:58
  115.4 10.1 %collective-permute-start.38 = (bf16[128,1152]{1,0:T(8,128)(2,1)S(1)}, bf16[128,1152]{1,0:T(8,128)(2,1)S(1)}, u32[]{:S(2)}, u32[]{:S(2)}) collective-permute-start(bf16[128,1152]{1,0:T(8,128)(2,1)S(1)} %add_convert_fusion.2), channel_id=1, source_target_pairs={{0,120},{1,121},{2,122},{3,123},{4,124},{5,125},{6,126},{7,127},{8... | collective-permute-start | bytes 884744 | tf_op jit(solution)/shard_map/ppermute | solution.py:58
  118.8 11.0 %collective-permute-start.39 = (bf16[128,1152]{1,0:T(8,128)(2,1)S(1)}, bf16[128,1152]{1,0:T(8,128)(2,1)S(1)}, u32[]{:S(2)}, u32[]{:S(2)}) collective-permute-start(bf16[128,1152]{1,0:T(8,128)(2,1)S(1)} %get-tuple-element.120), channel_id=1, source_target_pairs={{0,96},{1,97},{2,98},{3,99},{4,100},{5,101},{6,102},{7,103},{8,104... | collective-permute-start | bytes 884744 | tf_op jit(solution)/shard_map/ppermute | solution.py:58
  120.2 9.7 %collective-permute-start.42 = (bf16[128,1152]{1,0:T(8,128)(2,1)S(1)}, bf16[128,1152]{1,0:T(8,128)(2,1)S(1)}, u32[]{:S(2)}, u32[]{:S(2)}) collective-permute-start(bf16[128,1152]{1,0:T(8,128)(2,1)S(1)} %add_convert_fusion.1), channel_id=1, source_target_pairs={{0,6},{1,7},{2,4},{3,5},{4,2},{5,3},{6,0},{7,1},{8,14},{9,15},{10,... | collective-permute-start | bytes 884744 | tf_op jit(solution)/shard_map/ppermute | solution.py:58
  (23 other events, 101.7 us)
where the time goes:
time: 131 us
  starting transfers between devices  46 us (35%)
  waiting for transfers between devices  45.5 us (35%)
  Pallas kernels  34.2 us (26%)
  other arithmetic  4.15 us (3%)
    ppermute x44, starting transfers between devices, swap(): return lax.ppermute(value, AXES, pairs(axes, kind))  46 us
    ppermute x44, waiting for transfers between devices, swap(): return lax.ppermute(value, AXES, pairs(axes, kind))  45.5 us
    pallas_call x10, Pallas kernels, call(): pl.pallas_call(body, out_shape=tuple((shape(*out) for out in outs)), in_s...  34.2 us
  transfers between devices with their start and end apart: 44, of which 24 were waited for; matrix products, arithmetic and copies ran while one was open for 2% of the time, Pallas kernels for 21%

commit v1 on v0

--- a/solution.py
+++ b/solution.py
@@ -204,7 +204,7 @@
 )
 
 
-LOOPS = (True, False, True, False)
+LOOPS = (True, False, False, False)
 
 
 def stage_kernel(stage, *refs):

time: 131 us -> 131 us (level)
  no operation moved by 1% of the time
where the time goes in v1:
time: 131 us; the launch traced here: 130 us
  starting transfers between devices  46.2 us (35%)
  waiting for transfers between devices  45.5 us (35%)
  Pallas kernels  33.7 us (26%)
  other arithmetic  4.15 us (3%)
    ppermute x44, starting transfers between devices, swap(): return lax.ppermute(value, AXES, pairs(axes, kind))  46.2 us
    ppermute x44, waiting for transfers between devices, swap(): return lax.ppermute(value, AXES, pairs(axes, kind))  45.5 us
    pallas_call x10, Pallas kernels, call(): pl.pallas_call(body, out_shape=tuple((shape(*out) for out in outs)), in_s...  33.7 us
  transfers between devices with their start and end apart: 44, of which 24 were waited for; matrix products, arithmetic and copies ran while one was open for 2% of the time, Pallas kernels for 21%

profile of v1, /device:TPU:0, one launch (start us, length us, event | category | flops | bytes accessed | tf_op | source)
XLA Modules:
  0.0 130.5 jit_solution(18440920687857338297)
XLA Ops:
  7.9 1.9 %collective-permute-start.5 = (bf16[528,1152]{1,0:T(8,128)(2,1)S(1)}, bf16[528,1152]{1,0:T(8,128)(2,1)S(1)}, u32[]{:S(2)}, u32[]{:S(2)}) collective-permute-start(bf16[528,1152]{1,0:T(8,128)(2,1)S(1)} %shard_map.94.refs_0_), channel_id=1, source_target_pairs={{0,32},{1,97},{2,34},{3,99},{4,36},{5,101},{6,38},{7,103},{8,40},{... | collective-permute-start | bytes 3649544 | tf_op jit(solution)/shard_map/ppermute | solution.py:58
  9.8 4.4 %collective-permute-start.9 = (bf16[528,1152]{1,0:T(8,128)(2,1)S(1)}, bf16[528,1152]{1,0:T(8,128)(2,1)S(1)}, u32[]{:S(2)}, u32[]{:S(2)}) collective-permute-start(bf16[528,1152]{1,0:T(8,128)(2,1)S(1)} %shard_map.94.refs_0_), channel_id=1, source_target_pairs={{0,1},{1,0},{2,3},{3,2},{4,5},{5,4},{6,7},{7,6},{8,9},{9,8},{10,11... | collective-permute-start | bytes 3649544 | tf_op jit(solution)/shard_map/ppermute | solution.py:58
  14.2 7.2 %collective-permute-done.7.refs_1_ = bf16[528,1152]{1,0:T(8,128)(2,1)S(1)} collective-permute-done((bf16[528,1152]{1,0:T(8,128)(2,1)S(1)}, bf16[528,1152]{1,0:T(8,128)(2,1)S(1)}, u32[]{:S(2)}, u32[]{:S(2)}) %collective-permute-start.7) | collective-permute-done | bytes 1216544 | tf_op jit(solution)/shard_map/ppermute | solution.py:58
  24.5 3.7 %collective-permute-start.12 = (bf16[528,1152]{1,0:T(8,128)(2,1)S(1)}, bf16[528,1152]{1,0:T(8,128)(2,1)S(1)}, u32[]{:S(2)}, u32[]{:S(2)}) collective-permute-start(bf16[528,1152]{1,0:T(8,128)(2,1)S(1)} %collective-permute-done.5.refs_3_), channel_id=1, source_target_pairs={{0,1},{1,0},{2,3},{3,2},{4,5},{5,4},{6,7},{7,6},{8,9},{9,8},{10,11... | collective-permute-start | bytes 3649544 | tf_op jit(solution)/shard_map/ppermute | solution.py:58
  28.6 2.1 %collective-permute-done.12.refs_7_ = bf16[528,1152]{1,0:T(8,128)(2,1)S(1)} collective-permute-done((bf16[528,1152]{1,0:T(8,128)(2,1)S(1)}, bf16[528,1152]{1,0:T(8,128)(2,1)S(1)}, u32[]{:S(2)}, u32[]{:S(2)}) %collective-permute-start.12) | collective-permute-done | bytes 1216544 | tf_op jit(solution)/shard_map/ppermute | solution.py:58
  30.7 5.5 %shard_map.95 = (bf16[1024,2048]{1,0:T(8,128)(2,1)S(1)}, f32[8,2048]{1,0:T(8,128)S(1)}, f32[8,2048]{1,0:T(8,128)S(1)}, bf16[2048,1152]{1,0:T(8,128)(2,1)S(1)}, b...) custom-call(bf16[528,1152]{1,0:T(8,128)(2,1)S(1)} %shard_map.94.refs_0_, ...), custom_call_target="tpu_custom_call" | custom-call | flops 2415919104 | bytes 8388608 | tf_op jit(solution)/shard_map/pallas_call | solution.py:297
  36.2 8.5 %collective-permute-done.6.yz.refs_1_ = bf16[528,1152]{1,0:T(8,128)(2,1)S(1)} collective-permute-done((bf16[528,1152]{1,0:T(8,128)(2,1)S(1)}, bf16[528,1152]{1,0:T(8,128)(2,1)S(1)}, u32[]{:S(2)}, u32[]{:S(2)}) %collective-permute-start.6) | collective-permute-done | bytes 1216544 | tf_op jit(solution)/shard_map/ppermute | solution.py:58
  45.3 2.7 %collective-permute-start.17 = (bf16[528,1152]{1,0:T(8,128)(2,1)S(1)}, bf16[528,1152]{1,0:T(8,128)(2,1)S(1)}, u32[]{:S(2)}, u32[]{:S(2)}) collective-permute-start(bf16[528,1152]{1,0:T(8,128)(2,1)S(1)} %collective-permute-done.16.refs_0_), channel_id=1, source_target_pairs={{0,1},{1,0},{2,3},{3,2},{4,5},{5,4},{6,7},{7,6},{8,9},{9,8},{10,11... | collective-permute-start | bytes 3649544 | tf_op jit(solution)/shard_map/ppermute | solution.py:58
  51.1 6.3 %shard_map.97 = (bf16[1024,2048]{1,0:T(8,128)(2,1)S(1)}, f32[8,2048]{1,0:T(8,128)S(1)}, f32[8,2048]{1,0:T(8,128)S(1)}, bf16[2048,1152]{1,0:T(8,128)(2,1)S(1)}, b...) custom-call(bf16[528,1152]{1,0:T(8,128)(2,1)S(1)} %collective-permut, ...), custom_call_target="tpu_custom_call", output_to_operand_aliasing={{0}: (6, {}), {1}: (7, {}), {2}: (8, {}), {3}: (9, {}), {4}... | custom-call | flops 3170893824 | bytes 8388608 | tf_op jit(solution)/shard_map/pallas_call | solution.py:297
  59.3 3.4 %shard_map.98 = (bf16[1024,2048]{1,0:T(8,128)(2,1)S(1)}, f32[8,2048]{1,0:T(8,128)S(1)}, f32[8,2048]{1,0:T(8,128)S(1)}, bf16[2048,1152]{1,0:T(8,128)(2,1)S(1)}, b...) custom-call(bf16[1024,2048]{1,0:T(8,128)(2,1)S(1)} %get-tuple-elemen, ...), custom_call_target="tpu_custom_call", output_to_operand_aliasing={{0}: (0, {}), {1}: (1, {}), {2}: (2, {}), {3}: (3, {}), {4}... | custom-call | flops 1811939328 | bytes 8388608 | tf_op jit(solution)/shard_map/pallas_call | solution.py:297
  62.7 5.5 %shard_map.99 = (bf16[1024,2048]{1,0:T(8,128)(2,1)S(1)}, f32[8,2048]{1,0:T(8,128)S(1)}, f32[8,2048]{1,0:T(8,128)S(1)}, bf16[2048,1152]{1,0:T(8,128)(2,1)S(1)}, b...) custom-call(bf16[272,1152]{1,0:T(8,128)(2,1)S(1)} %collective-permut, ...), custom_call_target="tpu_custom_call", output_to_operand_aliasing={{0}: (4, {}), {1}: (5, {}), {2}: (6, {}), {3}: (7, {}), {4}... | custom-call | flops 2264924160 | bytes 8388608 | tf_op jit(solution)/shard_map/pallas_call | solution.py:297
  70.8 2.4 %collective-permute-done.23 = f32[8,128]{1,0:T(8,128)S(1)} collective-permute-done((f32[8,128]{1,0:T(8,128)S(1)}, f32[8,128]{1,0:T(8,128)S(1)}, u32[]{:S(2)}, u32[]{:S(2)}) %collective-permute-start.23) | collective-permute-done | bytes 4128 | tf_op jit(solution)/shard_map/ppermute | solution.py:58
  75.1 3.2 %shard_map.100 = bf16[1024,1152]{1,0:T(8,128)(2,1)S(1)} custom-call(bf16[1024,2048]{1,0:T(8,128)(2,1)S(1)} %get-tuple-element.92.grad, bf16[1024,1152]{1,0:T(8,128)(2,1)S(1)} %get-tuple-element.97.txt), custom_call_target="tpu_custom_call" | custom-call | flops 2415919104 | bytes 6291456 | tf_op jit(solution)/shard_map/pallas_call | solution.py:297
  78.4 3.2 %shard_map.101.mine = bf16[1024,1152]{1,0:T(8,128)(2,1)S(1)} custom-call(bf16[1024,2048]{1,0:T(8,128)(2,1)S(1)} %get-tuple-element.92.grad, bf16[1024,1152]{1,0:T(8,128)(2,1)S(1)} %get-tuple-element.97.txt), custom_call_target="tpu_custom_call" | custom-call | flops 2415919104 | bytes 6291456 | tf_op jit(solution)/shard_map/pallas_call | solution.py:297
  82.0 2.4 %collective-permute-start.27 = (f32[8,128]{1,0:T(8,128)S(1)}, f32[8,128]{1,0:T(8,128)S(1)}, u32[]{:S(2)}, u32[]{:S(2)}) collective-permute-start(f32[8,128]{1,0:T(8,128)S(1)} %add.73), channel_id=1, source_target_pairs={{0,24},{1,25},{2,26},{3,27},{4,28},{5,29},{6,30},{7,31},{8,16},{9,... | collective-permute-start | bytes 12296 | tf_op jit(solution)/shard_map/ppermute | solution.py:58
  84.5 2.4 %collective-permute-done.27 = f32[8,128]{1,0:T(8,128)S(1)} collective-permute-done((f32[8,128]{1,0:T(8,128)S(1)}, f32[8,128]{1,0:T(8,128)S(1)}, u32[]{:S(2)}, u32[]{:S(2)}) %collective-permute-start.27) | collective-permute-done | bytes 4128 | tf_op jit(solution)/shard_map/ppermute | solution.py:58
  86.9 3.6 %collective-permute-done.34 = f32[8,128]{1,0:T(8,128)S(1)} collective-permute-done((f32[8,128]{1,0:T(8,128)S(1)}, f32[8,128]{1,0:T(8,128)S(1)}, u32[]{:S(2)}, u32[]{:S(2)}) %collective-permute-start.34) | collective-permute-done | bytes 4128 | tf_op jit(solution)/shard_map/ppermute | solution.py:58
  96.2 5.9 %shard_map.103 = (bf16[128,1152]{1,0:T(8,128)(2,1)S(1)}, bf16[128,1152]{1,0:T(8,128)(2,1)S(1)}, bf16[128,1152]{1,0:T(8,128)(2,1)S(1)}, bf16[128,1152]{1,0:T(8,12...) custom-call(f32[8,128]{1,0:T(8,128)S(1)} %add.81.score, ...), custom_call_target="tpu_custom_call" | custom-call | flops 4831838208 | bytes 12582912 | tf_op jit(solution)/shard_map/pallas_call | solution.py:297
  103.8 2.5 %collective-permute-start.40 = (bf16[128,1152]{1,0:T(8,128)(2,1)S(1)}, bf16[128,1152]{1,0:T(8,128)(2,1)S(1)}, u32[]{:S(2)}, u32[]{:S(2)}) collective-permute-start(bf16[128,1152]{1,0:T(8,128)(2,1)S(1)} %get-tuple-element.123), channel_id=1, source_target_pairs={{0,24},{1,25},{2,26},{3,27},{4,28},{5,29},{6,30},{7,31},{8,16},{9,... | collective-permute-start | bytes 884744 | tf_op jit(solution)/shard_map/ppermute | solution.py:58
  111.3 2.8 %collective-permute-done.40 = bf16[128,1152]{1,0:T(8,128)(2,1)S(1)} collective-permute-done((bf16[128,1152]{1,0:T(8,128)(2,1)S(1)}, bf16[128,1152]{1,0:T(8,128)(2,1)S(1)}, u32[]{:S(2)}, u32[]{:S(2)}) %collective-permute-start.40) | collective-permute-done | bytes 294944 | tf_op jit(solution)/shard_map/ppermute | solution.py:58
  115.1 2.5 %collective-permute-start.38 = (bf16[128,1152]{1,0:T(8,128)(2,1)S(1)}, bf16[128,1152]{1,0:T(8,128)(2,1)S(1)}, u32[]{:S(2)}, u32[]{:S(2)}) collective-permute-start(bf16[128,1152]{1,0:T(8,128)(2,1)S(1)} %add_convert_fusion.2), channel_id=1, source_target_pairs={{0,120},{1,121},{2,122},{3,123},{4,124},{5,125},{6,126},{7,127},{8... | collective-permute-start | bytes 884744 | tf_op jit(solution)/shard_map/ppermute | solution.py:58
  120.0 1.9 %collective-permute-start.42 = (bf16[128,1152]{1,0:T(8,128)(2,1)S(1)}, bf16[128,1152]{1,0:T(8,128)(2,1)S(1)}, u32[]{:S(2)}, u32[]{:S(2)}) collective-permute-start(bf16[128,1152]{1,0:T(8,128)(2,1)S(1)} %add_convert_fusion.1), channel_id=1, source_target_pairs={{0,6},{1,7},{2,4},{3,5},{4,2},{5,3},{6,0},{7,1},{8,14},{9,15},{10,... | collective-permute-start | bytes 884744 | tf_op jit(solution)/shard_map/ppermute | solution.py:58
  122.7 2.5 %collective-permute-done.38 = bf16[128,1152]{1,0:T(8,128)(2,1)S(1)} collective-permute-done((bf16[128,1152]{1,0:T(8,128)(2,1)S(1)}, bf16[128,1152]{1,0:T(8,128)(2,1)S(1)}, u32[]{:S(2)}, u32[]{:S(2)}) %collective-permute-start.38) | collective-permute-done | bytes 294944 | tf_op jit(solution)/shard_map/ppermute | solution.py:58
  125.2 4.3 %collective-permute-done.39 = bf16[128,1152]{1,0:T(8,128)(2,1)S(1)} collective-permute-done((bf16[128,1152]{1,0:T(8,128)(2,1)S(1)}, bf16[128,1152]{1,0:T(8,128)(2,1)S(1)}, u32[]{:S(2)}, u32[]{:S(2)}) %collective-permute-start.39) | collective-permute-done | bytes 294944 | tf_op jit(solution)/shard_map/ppermute | solution.py:58
  (100 shorter events, 38.8 us)
Async XLA Ops:
  4.7 16.7 %collective-permute-start.7 = (bf16[528,1152]{1,0:T(8,128)(2,1)S(1)}, bf16[528,1152]{1,0:T(8,128)(2,1)S(1)}, u32[]{:S(2)}, u32[]{:S(2)}) collective-permute-start(bf16[528,1152]{1,0:T(8,128)(2,1)S(1)} %shard_map.94.refs_0_), channel_id=1, source_target_pairs={{0,2},{1,7},{2,0},{3,5},{4,6},{5,3},{6,4},{7,1},{8,10},{9,15},{10,... | collective-permute-start | bytes 3649544 | tf_op jit(solution)/shard_map/ppermute | solution.py:58
  6.3 16.6 %collective-permute-start.8 = (bf16[528,1152]{1,0:T(8,128)(2,1)S(1)}, bf16[528,1152]{1,0:T(8,128)(2,1)S(1)}, u32[]{:S(2)}, u32[]{:S(2)}) collective-permute-start(bf16[528,1152]{1,0:T(8,128)(2,1)S(1)} %shard_map.94.refs_0_), channel_id=1, source_target_pairs={{0,8},{1,25},{2,10},{3,27},{4,12},{5,29},{6,14},{7,31},{8,0},{9,17... | collective-permute-start | bytes 3649544 | tf_op jit(solution)/shard_map/ppermute | solution.py:58
  7.9 16.6 %collective-permute-start.5 = (bf16[528,1152]{1,0:T(8,128)(2,1)S(1)}, bf16[528,1152]{1,0:T(8,128)(2,1)S(1)}, u32[]{:S(2)}, u32[]{:S(2)}) collective-permute-start(bf16[528,1152]{1,0:T(8,128)(2,1)S(1)} %shard_map.94.refs_0_), channel_id=1, source_target_pairs={{0,32},{1,97},{2,34},{3,99},{4,36},{5,101},{6,38},{7,103},{8,40},{... | collective-permute-start | bytes 3649544 | tf_op jit(solution)/shard_map/ppermute | solution.py:58
  9.8 18.5 %collective-permute-start.9 = (bf16[528,1152]{1,0:T(8,128)(2,1)S(1)}, bf16[528,1152]{1,0:T(8,128)(2,1)S(1)}, u32[]{:S(2)}, u32[]{:S(2)}) collective-permute-start(bf16[528,1152]{1,0:T(8,128)(2,1)S(1)} %shard_map.94.refs_0_), channel_id=1, source_target_pairs={{0,1},{1,0},{2,3},{3,2},{4,5},{5,4},{6,7},{7,6},{8,9},{9,8},{10,11... | collective-permute-start | bytes 3649544 | tf_op jit(solution)/shard_map/ppermute | solution.py:58
  28.2 16.6 %collective-permute-start.6 = (bf16[528,1152]{1,0:T(8,128)(2,1)S(1)}, bf16[528,1152]{1,0:T(8,128)(2,1)S(1)}, u32[]{:S(2)}, u32[]{:S(2)}) collective-permute-start(bf16[528,1152]{1,0:T(8,128)(2,1)S(1)} %collective-permute-done.5.refs_3_), channel_id=1, source_target_pairs={{0,8},{1,25},{2,10},{3,27},{4,12},{5,29},{6,14},{7,31},{8,0},{9,17... | collective-permute-start | bytes 3649544 | tf_op jit(solution)/shard_map/ppermute | solution.py:58
  28.3 16.6 %collective-permute-start.13 = (bf16[528,1152]{1,0:T(8,128)(2,1)S(1)}, bf16[528,1152]{1,0:T(8,128)(2,1)S(1)}, u32[]{:S(2)}, u32[]{:S(2)}) collective-permute-start(bf16[528,1152]{1,0:T(8,128)(2,1)S(1)} %collective-permute-done.7.refs_1_), channel_id=1, source_target_pairs={{0,32},{1,97},{2,34},{3,99},{4,36},{5,101},{6,38},{7,103},{8,40},{... | collective-permute-start | bytes 3649544 | tf_op jit(solution)/shard_map/ppermute | solution.py:58
  28.3 17.0 %collective-permute-start.16 = (bf16[528,1152]{1,0:T(8,128)(2,1)S(1)}, bf16[528,1152]{1,0:T(8,128)(2,1)S(1)}, u32[]{:S(2)}, u32[]{:S(2)}) collective-permute-start(bf16[528,1152]{1,0:T(8,128)(2,1)S(1)} %collective-permute-done.8.refs_2_), channel_id=1, source_target_pairs={{0,2},{1,7},{2,0},{3,5},{4,6},{5,3},{6,4},{7,1},{8,10},{9,15},{10,... | collective-permute-start | bytes 3649544 | tf_op jit(solution)/shard_map/ppermute | solution.py:58
  48.1 10.4 %collective-permute-start.14 = (bf16[272,1152]{1,0:T(8,128)(2,1)S(1)}, bf16[272,1152]{1,0:T(8,128)(2,1)S(1)}, u32[]{:S(2)}, u32[]{:S(2)}) collective-permute-start(bf16[272,1152]{1,0:T(8,128)(2,1)S(1)} %get-tuple-element.68), channel_id=1, source_target_pairs={{0,2},{1,7},{2,0},{3,5},{4,6},{5,3},{6,4},{7,1},{8,10},{9,15},{10,... | collective-permute-start | bytes 1880072 | tf_op jit(solution)/shard_map/ppermute | solution.py:58
  48.2 10.1 %collective-permute-start.15 = (bf16[256,1152]{1,0:T(8,128)(2,1)S(1)}, bf16[256,1152]{1,0:T(8,128)(2,1)S(1)}, u32[]{:S(2)}, u32[]{:S(2)}) collective-permute-start(bf16[256,1152]{1,0:T(8,128)(2,1)S(1)} %get-tuple-element.69), channel_id=1, source_target_pairs={{0,8},{1,25},{2,10},{3,27},{4,12},{5,29},{6,14},{7,31},{8,0},{9,17... | collective-permute-start | bytes 1769480 | tf_op jit(solution)/shard_map/ppermute | solution.py:58
  78.3 12.2 %collective-permute-start.25 = (bf16[1024,1152]{1,0:T(8,128)(2,1)S(1)}, bf16[1024,1152]{1,0:T(8,128)(2,1)S(1)}, u32[]{:S(2)}, u32[]{:S(2)}) collective-permute-start(bf16[1024,1152]{1,0:T(8,128)(2,1)S(1)} %shard_map.100), channel_id=1, source_target_pairs={{0,1},{1,0},{2,3},{3,2},{4,5},{5,4},{6,7},{7,6},{8,9},{9,8},{10,11... | collective-permute-start | bytes 7077896 | tf_op jit(solution)/shard_map/ppermute | solution.py:58
  92.5 11.2 %collective-permute-start.30 = (bf16[128,1152]{1,0:T(8,128)(2,1)S(1)}, bf16[128,1152]{1,0:T(8,128)(2,1)S(1)}, u32[]{:S(2)}, u32[]{:S(2)}) collective-permute-start(bf16[128,1152]{1,0:T(8,128)(2,1)S(1)} %get-tuple-element.104), channel_id=1, source_target_pairs={{0,32},{1,33},{2,34},{3,35},{4,36},{5,37},{6,38},{7,39},{8,40},{9,... | collective-permute-start | bytes 884744 | tf_op jit(solution)/shard_map/ppermute | solution.py:58
  93.6 12.7 %collective-permute-start.28 = (bf16[128,1152]{1,0:T(8,128)(2,1)S(1)}, bf16[128,1152]{1,0:T(8,128)(2,1)S(1)}, u32[]{:S(2)}, u32[]{:S(2)}) collective-permute-start(bf16[128,1152]{1,0:T(8,128)(2,1)S(1)} %get-tuple-element.103), channel_id=1, source_target_pairs={{0,2},{1,3},{2,0},{3,1},{4,6},{5,7},{6,4},{7,5},{8,10},{9,11},{10,... | collective-permute-start | bytes 884744 | tf_op jit(solution)/shard_map/ppermute | solution.py:58
  93.8 13.9 %collective-permute-start.31 = (bf16[128,1152]{1,0:T(8,128)(2,1)S(1)}, bf16[128,1152]{1,0:T(8,128)(2,1)S(1)}, u32[]{:S(2)}, u32[]{:S(2)}) collective-permute-start(bf16[128,1152]{1,0:T(8,128)(2,1)S(1)} %get-tuple-element.107), channel_id=1, source_target_pairs={{0,8},{1,9},{2,10},{3,11},{4,12},{5,13},{6,14},{7,15},{8,0},{9,1},... | collective-permute-start | bytes 884744 | tf_op jit(solution)/shard_map/ppermute | solution.py:58
  93.8 14.9 %collective-permute-start.32 = (bf16[128,1152]{1,0:T(8,128)(2,1)S(1)}, bf16[128,1152]{1,0:T(8,128)(2,1)S(1)}, u32[]{:S(2)}, u32[]{:S(2)}) collective-permute-start(bf16[128,1152]{1,0:T(8,128)(2,1)S(1)} %get-tuple-element.108), channel_id=1, source_target_pairs={{0,32},{1,33},{2,34},{3,35},{4,36},{5,37},{6,38},{7,39},{8,40},{9,... | collective-permute-start | bytes 884744 | tf_op jit(solution)/shard_map/ppermute | solution.py:58
  102.1 8.0 %collective-permute-start.37 = (bf16[128,1152]{1,0:T(8,128)(2,1)S(1)}, bf16[128,1152]{1,0:T(8,128)(2,1)S(1)}, u32[]{:S(2)}, u32[]{:S(2)}) collective-permute-start(bf16[128,1152]{1,0:T(8,128)(2,1)S(1)} %get-tuple-element.118), channel_id=1, source_target_pairs={{0,6},{1,7},{2,4},{3,5},{4,2},{5,3},{6,0},{7,1},{8,14},{9,15},{10,... | collective-permute-start | bytes 884744 | tf_op jit(solution)/shard_map/ppermute | solution.py:58
  103.8 10.4 %collective-permute-start.40 = (bf16[128,1152]{1,0:T(8,128)(2,1)S(1)}, bf16[128,1152]{1,0:T(8,128)(2,1)S(1)}, u32[]{:S(2)}, u32[]{:S(2)}) collective-permute-start(bf16[128,1152]{1,0:T(8,128)(2,1)S(1)} %get-tuple-element.123), channel_id=1, source_target_pairs={{0,24},{1,25},{2,26},{3,27},{4,28},{5,29},{6,30},{7,31},{8,16},{9,... | collective-permute-start | bytes 884744 | tf_op jit(solution)/shard_map/ppermute | solution.py:58
  106.3 8.9 %collective-permute-start.41 = (bf16[128,1152]{1,0:T(8,128)(2,1)S(1)}, bf16[128,1152]{1,0:T(8,128)(2,1)S(1)}, u32[]{:S(2)}, u32[]{:S(2)}) collective-permute-start(bf16[128,1152]{1,0:T(8,128)(2,1)S(1)} %get-tuple-element.124), channel_id=1, source_target_pairs={{0,96},{1,97},{2,98},{3,99},{4,100},{5,101},{6,102},{7,103},{8,104... | collective-permute-start | bytes 884744 | tf_op jit(solution)/shard_map/ppermute | solution.py:58
  107.7 12.2 %collective-permute-start.36 = (bf16[128,1152]{1,0:T(8,128)(2,1)S(1)}, bf16[128,1152]{1,0:T(8,128)(2,1)S(1)}, u32[]{:S(2)}, u32[]{:S(2)}) collective-permute-start(bf16[128,1152]{1,0:T(8,128)(2,1)S(1)} %get-tuple-element.114), channel_id=1, source_target_pairs={{0,8},{1,9},{2,10},{3,11},{4,12},{5,13},{6,14},{7,15},{8,0},{9,1},... | collective-permute-start | bytes 884744 | tf_op jit(solution)/shard_map/ppermute | solution.py:58
  108.7 21.0 %collective-permute-start.43 = (bf16[128,1152]{1,0:T(8,128)(2,1)S(1)}, bf16[128,1152]{1,0:T(8,128)(2,1)S(1)}, u32[]{:S(2)}, u32[]{:S(2)}) collective-permute-start(bf16[128,1152]{1,0:T(8,128)(2,1)S(1)} %get-tuple-element.126), channel_id=1, source_target_pairs={{0,24},{1,25},{2,26},{3,27},{4,28},{5,29},{6,30},{7,31},{8,16},{9,... | collective-permute-start | bytes 884744 | tf_op jit(solution)/shard_map/ppermute | solution.py:58
  110.1 8.5 %collective-permute-start.29 = (bf16[128,1152]{1,0:T(8,128)(2,1)S(1)}, bf16[128,1152]{1,0:T(8,128)(2,1)S(1)}, u32[]{:S(2)}, u32[]{:S(2)}) collective-permute-start(bf16[128,1152]{1,0:T(8,128)(2,1)S(1)} %add_convert_fusion.4), channel_id=1, source_target_pairs={{0,40},{1,41},{2,42},{3,43},{4,44},{5,45},{6,46},{7,47},{8,32},{9,... | collective-permute-start | bytes 884744 | tf_op jit(solution)/shard_map/ppermute | solution.py:58
  114.1 7.7 %collective-permute-start.33 = (bf16[128,1152]{1,0:T(8,128)(2,1)S(1)}, bf16[128,1152]{1,0:T(8,128)(2,1)S(1)}, u32[]{:S(2)}, u32[]{:S(2)}) collective-permute-start(bf16[128,1152]{1,0:T(8,128)(2,1)S(1)} %add_convert_fusion.3), channel_id=1, source_target_pairs={{0,2},{1,3},{2,0},{3,1},{4,6},{5,7},{6,4},{7,5},{8,10},{9,11},{10,... | collective-permute-start | bytes 884744 | tf_op jit(solution)/shard_map/ppermute | solution.py:58
  115.1 10.1 %collective-permute-start.38 = (bf16[128,1152]{1,0:T(8,128)(2,1)S(1)}, bf16[128,1152]{1,0:T(8,128)(2,1)S(1)}, u32[]{:S(2)}, u32[]{:S(2)}) collective-permute-start(bf16[128,1152]{1,0:T(8,128)(2,1)S(1)} %add_convert_fusion.2), channel_id=1, source_target_pairs={{0,120},{1,121},{2,122},{3,123},{4,124},{5,125},{6,126},{7,127},{8... | collective-permute-start | bytes 884744 | tf_op jit(solution)/shard_map/ppermute | solution.py:58
  118.6 11.0 %collective-permute-start.39 = (bf16[128,1152]{1,0:T(8,128)(2,1)S(1)}, bf16[128,1152]{1,0:T(8,128)(2,1)S(1)}, u32[]{:S(2)}, u32[]{:S(2)}) collective-permute-start(bf16[128,1152]{1,0:T(8,128)(2,1)S(1)} %get-tuple-element.120), channel_id=1, source_target_pairs={{0,96},{1,97},{2,98},{3,99},{4,100},{5,101},{6,102},{7,103},{8,104... | collective-permute-start | bytes 884744 | tf_op jit(solution)/shard_map/ppermute | solution.py:58
  120.0 9.7 %collective-permute-start.42 = (bf16[128,1152]{1,0:T(8,128)(2,1)S(1)}, bf16[128,1152]{1,0:T(8,128)(2,1)S(1)}, u32[]{:S(2)}, u32[]{:S(2)}) collective-permute-start(bf16[128,1152]{1,0:T(8,128)(2,1)S(1)} %add_convert_fusion.1), channel_id=1, source_target_pairs={{0,6},{1,7},{2,4},{3,5},{4,2},{5,3},{6,0},{7,1},{8,14},{9,15},{10,... | collective-permute-start | bytes 884744 | tf_op jit(solution)/shard_map/ppermute | solution.py:58
  (23 other events, 100.9 us)
